TPU v7x, 128 devices: a whole 4x4x4 slice. The times are simulated.
128 devices in a mesh: gx: 4 (over x), gy: 4 (over z_hi, core), gz: 8 (over z_lo, y).
Axes of the slice: x: 4, y: 4, z: 4 (z_hi: 2, z_lo: 2; z = z_hi * 2 + z_lo), core: 2. Of those that a mesh axis runs over, the one named last changes fastest.
Arguments:
- right_side: float32 [3, 64, 64, 1024], P(None, 'gx', 'gy', 'gz'), may hold values from -24 to 24
- labels: int32 [64, 64, 1024], P('gx', 'gy', 'gz'), may hold values from 0 to 15
- colors: int32 [3, 64, 64, 1024], P(None, 'gx', 'gy', 'gz'), may hold values from 0 to 3
- table: float32 [16], replicated, may hold values from 0.5 to 4
Outputs:
- preconditioned: float32 [3, 64, 64, 1024], P(None, 'gx', 'gy', 'gz')
All inputs are finite; a program needn't handle non-finite values.
Results may differ from a plain program's by a relative error of at most 0.00002.
Values sent between devices are 32-bit elements; how exact they have to be, the bound alone decides.
A program may use at most 64 MiB of HBM per device.

v0:
```python
import functools
import itertools

import jax
import jax.numpy as jnp
from jax import lax
from jax.experimental import pallas as pl
from jax.experimental.pallas import tpu as pltpu
from jax.sharding import PartitionSpec as P

NSWEEP = 2
NCOL = 4
NCHEB = 4
AXES = ("gx", "gy", "gz")

H = 4
N = 16
B = N + 2 * H
LANES = 128
OWN = slice(H, H + N)
DIRS = [d for d in itertools.product((-1, 0, 1), repeat=3) if d != (0, 0, 0)]


def roll(values, shift, axis):
    return pltpu.roll(values, shift, axis)


def down_lane(values):
    return roll(values, 1, 1)


def up_lane(values):
    return roll(values, LANES - 1, 1)


def down_row(values):
    return roll(values, 1, 0)


def up_row(values):
    return roll(values, B - 1, 0)


def group_of(xp):
    ring = lax.rem(xp + (B - H), B)
    return ring // 8, lax.rem(ring, 8)


def select_table(labels, table):
    level = [table[i] for i in range(16)]
    for bit in range(4):
        odd = (labels & (1 << bit)) != 0
        level = [jnp.where(odd, level[i + 1], level[i]) for i in range(0, len(level), 2)]
    return level[0]


def kernel(
    sizes,
    r_hbm, lab_hbm, col_hbm, tab,
    out,
    r_in, lab_in, col_in,
    W, QM, QR, PW, INV, PINV, PMASK, PKEEP,
    E, PE, E2, PE2, QME, QRE, U,
    NR, ND, NY, PR, PD, PY, UD,
    in_sem, ssem, rsem,
):
    here = [lax.axis_index(a) for a in AXES]

    def neighbour(d):
        return tuple(lax.rem(here[i] + (d[i] + sizes[i]), sizes[i]) for i in range(3))

    barrier = pltpu.get_barrier_semaphore()
    for d in DIRS:
        pl.semaphore_signal(barrier, inc=1, device_id=neighbour(d), device_id_type=pl.DeviceIdType.MESH)
    loads = [
        pltpu.make_async_copy(src, dst, in_sem.at[i])
        for i, (src, dst) in enumerate(((lab_hbm, lab_in), (r_hbm, r_in), (col_hbm, col_in)))
    ]
    for load in loads:
        load.start()

    first = [jnp.where(here[i] > 0, 1.0, 0.0).astype(jnp.float32) for i in range(3)]
    last = [jnp.where(here[i] < sizes[i] - 1, 1.0, 0.0).astype(jnp.float32) for i in range(3)]
    lane = lax.broadcasted_iota(jnp.int32, (B, LANES), 1)
    row = lax.broadcasted_iota(jnp.int32, (B, LANES), 0)
    spot = lane % 16
    low_rows = jnp.where(row < H, first[1], 1.0)
    row_mask = low_rows * jnp.where(row >= H + N, last[1], 1.0)
    low_ends = jnp.where((spot >= 8) & (spot < 12), first[2], 1.0) * low_rows
    ends = jnp.where((spot >= 4) & (spot < 8), last[2], 1.0) * low_ends * jnp.where(
        row >= H + N, last[1], 1.0
    )
    before = jnp.where(lane >= 64, first[0], 1.0)
    after = jnp.where(lane < 64, last[0], 1.0)
    for t in range(3):
        PKEEP[t] = low_ends * before if t == 2 else low_ends
        PMASK[t] = ends * before * after if t == 2 else ends

    def x_low(xp):
        return jnp.where(xp >= H, 1.0, first[0])

    def x_mask(xp):
        return x_low(xp) * jnp.where(xp < H + N, 1.0, last[0])

    for load in loads:
        load.wait()

    @pl.loop(0, N)
    def _(x):
        W[3, x + H, OWN] = select_table(lab_in[x], tab)
        for c in range(3):
            W[c, x + H, OWN] = r_in[c, x]
            W[4 + c, x + H, OWN] = col_in[c, x].astype(jnp.float32) + 1.0

    def pack_own(src, dst, fields):
        narrow = lax.broadcasted_iota(jnp.int32, (N, LANES), 1) // 16

        @pl.loop(0, fields)
        def _(f):
            for t in range(2):
                total = None
                for g in range(8):
                    piece = roll(src[f, H + 8 * t + g, OWN], 16 * g + 4, 1)
                    total = piece if g == 0 else jnp.where(narrow == g, piece, total)
                dst[f, t, OWN] = total

    pack_own(W, QM, 7)
    pl.semaphore_wait(barrier, len(DIRS))

    def span(d, side):
        if d == 0:
            return slice(H, H + N)
        low = (d > 0) == (side == "dst")
        if side == "dst":
            return slice(0, H) if low else slice(H + N, B)
        return slice(H, 2 * H) if d < 0 else slice(N, N + H)

    def exchange(phase, main, packed, received):
        copies = []
        for i, d in enumerate(DIRS):
            rows_src, rows_dst = span(d[1], "src"), span(d[1], "dst")
            if d[2] == 0:
                src = main.at[:, span(d[0], "src"), rows_src]
                dst = main.at[:, span(d[0], "dst"), rows_dst]
            else:
                slot_src = {0: slice(0, 2), 1: slice(1, 2), -1: slice(0, 1)}[d[0]]
                slot_dst = {0: slice(0, 2), 1: slice(3, 4), -1: slice(2, 3)}[d[0]]
                src = packed.at[:, slot_src, rows_src]
                dst = received.at[1 if d[2] > 0 else 0, :, slot_dst, rows_dst]
            copies.append(
                pltpu.make_async_remote_copy(
                    src_ref=src,
                    dst_ref=dst,
                    send_sem=ssem.at[phase, i],
                    recv_sem=rsem.at[phase, i],
                    device_id=neighbour(d),
                    device_id_type=pl.DeviceIdType.MESH,
                )
            )
        order = sorted(range(len(DIRS)), key=lambda i: (-abs(DIRS[i][0]), sum(map(abs, DIRS[i]))))
        for i in order:
            copies[i].start()
        return copies

    def assemble(src, received, dst, fields):
        @pl.loop(0, fields)
        def _(f):
            for t in range(3):
                own = None
                for g in range(8):
                    x = (8 * t + g + H) % B
                    piece = roll(src[f, x], 16 * g + 4, 1)
                    own = piece if g == 0 else jnp.where(lane // 16 == g, piece, own)
                if t < 2:
                    high, low = received[0, f, t], received[1, f, t]
                else:
                    high = jnp.where(lane < 64, received[0, f, 2], received[0, f, 3])
                    low = jnp.where(lane < 64, received[1, f, 2], received[1, f, 3])
                upper = jnp.where(spot < 4, own, high)
                lower = roll(jnp.where(spot < 4, low, own), 8, 1)
                dst[f, t] = jnp.where(PMASK[t] > 0.0, jnp.where(spot < 8, upper, lower), 0.0)

    copies = exchange(0, W, QM, QR)
    for copy in copies:
        copy.wait()

    @pl.loop(0, B)
    def _(xp):
        inside = (row_mask * x_mask(xp)) > 0.0
        for f in range(7):
            W[f, xp] = jnp.where(inside, W[f, xp], 0.0)
        inverse = 1.0 / (16.0 + W[3, xp])
        INV[xp] = inverse
        for c in range(3):
            E[c, xp] = jnp.where(W[4 + c, xp] == 1.0, W[c, xp] * inverse, 0.0)

    assemble(W, QR, PW, 7)
    for t in range(3):
        PINV[t] = 1.0 / (16.0 + PW[3, t])
        for c in range(3):
            PE[c, t] = jnp.where(PW[4 + c, t] == 1.0, PW[c, t] * PINV[t], 0.0)

    def next_plane(tiles):
        moved = [roll(v, LANES - 16, 1) for v in tiles]
        return [jnp.where(lane < LANES - 16, moved[t], moved[(t + 1) % 3]) for t in range(3)]

    def previous_plane(tiles):
        moved = [roll(v, 16, 1) for v in tiles]
        return [jnp.where(lane >= 16, moved[t], moved[(t + 2) % 3]) for t in range(3)]

    def packed_turn(colour, edges):
        ex, ey, ez = ([edges[c, t] for t in range(3)] for c in range(3))
        eyx, ezx = next_plane(ey), next_plane(ez)
        fx, fy, fz = [], [], []
        for t in range(3):
            keep = PKEEP[t]
            fx.append((ey[t] - up_lane(ey[t]) + up_row(ez[t]) - ez[t]) * keep)
            fy.append((ez[t] - ezx[t] + up_lane(ex[t]) - ex[t]) * keep)
            fz.append((ex[t] - up_row(ex[t]) + eyx[t] - ey[t]) * keep)
        fyp, fzp = previous_plane(fy), previous_plane(fz)
        for t in range(3):
            U[0, t] = jnp.where(spot == 4, ex[t], roll(fy[t], LANES - 6, 1))
            U[1, t] = jnp.where(spot == 4, ey[t], roll(fx[t], LANES - 6, 1))
            back = (
                fz[t] - down_row(fz[t]) - fy[t] + down_lane(fy[t]),
                fx[t] - down_lane(fx[t]) - fz[t] + fzp[t],
                fy[t] - fyp[t] - fx[t] + down_row(fx[t]),
            )
            for c, old in enumerate((ex[t], ey[t], ez[t])):
                residual = PW[c, t] - back[c] - PW[3, t] * old
                edges[c, t] = old + jnp.where(PW[4 + c, t] == colour + 1.0, residual * PINV[t], 0.0)

    def turn(colour, edges, packed, reach, target=None):
        packed_turn(colour, packed)

        def faces(xp):
            t, g = group_of(xp)
            shift = lax.rem(251 - 16 * g, LANES)
            end_x, end_y = roll(U[0, t], shift, 1), roll(U[1, t], shift, 1)
            ex, ey, ez = (edges[c, xp] for c in range(3))
            ex_z = jnp.where(lane == LANES - 1, end_x, up_lane(ex))
            ey_z = jnp.where(lane == LANES - 1, end_y, up_lane(ey))
            keep = low_rows * x_low(xp)
            fx = (ey - ey_z + up_row(ez) - ez) * keep
            fy = (ez - edges[2, xp + 1] + ex_z - ex) * keep
            fz = (ex - up_row(ex) + edges[1, xp + 1] - ey) * keep
            return fx, fy, fz, end_x, end_y, (ex, ey, ez)

        def body(xp, carry):
            fyp, fzp = carry
            fx, fy, fz, end_x, end_y, old = faces(xp)
            fx_z = jnp.where(lane == 0, end_y, down_lane(fx))
            fy_z = jnp.where(lane == 0, end_x, down_lane(fy))
            back = (
                fz - down_row(fz) - fy + fy_z,
                fx - fx_z - fz + fzp,
                fy - fyp - fx + down_row(fx),
            )
            sigma, inverse = W[3, xp], INV[xp]
            for c in range(3):
                residual = W[c, xp] - back[c] - sigma * old[c]
                value = old[c] + jnp.where(W[4 + c, xp] == colour + 1.0, residual * inverse, 0.0)
                if target is None:
                    edges[c, xp] = value
                else:
                    target[c, xp, OWN] = value[OWN]
            return fy, fz

        start = faces(H - reach - 1)
        lax.fori_loop(H - reach, H + N + reach, body, (start[1], start[2]))

    turn(1, E, PE, 2)
    turn(2, E, PE, 1)
    turn(3, E, PE, 0, target=E2)

    pack_own(E2, QME, 3)
    copies = exchange(1, E2, QME, QRE)

    top = tab[0]
    for i in range(1, 16):
        top = jnp.maximum(top, tab[i])
    upper = jnp.full((B, LANES), 13.0 * top, jnp.float32)
    ratio = 31.0 / 29.0
    per_centre = (60.0 / 31.0) / upper
    per_half = (60.0 / 29.0) / upper

    @pl.loop(1, B)
    def _(xp):
        t, g = group_of(xp)
        end = roll(PW[2, t], lax.rem(245 - 16 * g, LANES), 1)
        inside = (row_mask * x_mask(xp)) > 0.0
        own = [W[c, xp] for c in range(3)]
        below = [W[0, xp - 1], down_row(own[1]), jnp.where(lane == 0, end, down_lane(own[2]))]
        values = [(below[0] - own[0]) + (below[1] - own[1]) + (below[2] - own[2])]
        values += [0.5 * (own[c] + below[c]) for c in range(3)]
        for f in range(4):
            value = jnp.where(inside, values[f], 0.0)
            NR[f, xp] = value
            value = value * per_centre
            ND[f, xp] = value
            NY[f, xp] = value

    own = [[PW[c, t] for t in range(3)] for c in range(3)]
    below = [
        previous_plane(own[0]),
        [down_row(v) for v in own[1]],
        [down_lane(v) for v in own[2]],
    ]
    for t in range(3):
        values = [sum((below[c][t] - own[c][t]) for c in range(3))]
        values += [0.5 * (own[c][t] + below[c][t]) for c in range(3)]
        for f in range(4):
            value = jnp.where(PMASK[t] > 0.0, values[f], 0.0)
            PR[f, t] = value
            value = value * per_centre
            PD[f, t] = value
            PY[f, t] = value

    rho = 1.0 / ratio
    for n in range(1, NCHEB):
        rho_next = 1.0 / (2.0 * ratio - rho)
        keep_part = rho_next * rho
        new_part = (2.0 * rho_next) * per_half
        rho = rho_next

        @pl.loop(0, 4)
        def _(f, keep_part=keep_part, new_part=new_part):
            mass = jnp.where(f > 0, 1.0, 0.0)
            d = [PD[f, t] for t in range(3)]
            dx = next_plane(d)
            sigma = [PW[3, t] for t in range(3)]
            wx = [sigma[t] * (dx[t] - d[t]) for t in range(3)]
            wxp = previous_plane(wx)
            for t in range(3):
                wy = sigma[t] * (up_row(d[t]) - d[t])
                wz = sigma[t] * (up_lane(d[t]) - d[t])
                UD[f, t] = jnp.where(spot == 4, d[t], roll(wz, LANES - 6, 1))
                applied = (
                    mass * sigma[t] * d[t]
                    + (wxp[t] - wx[t]) + (down_row(wy) - wy) + (down_lane(wz) - wz)
                )
                res = PR[f, t] - applied
                PR[f, t] = res
                new = jnp.where(PMASK[t] > 0.0, keep_part * d[t] + new_part * res, 0.0)
                PD[f, t] = new
                PY[f, t] = PY[f, t] + new

        def node_body(xp, carry, keep_part=keep_part, new_part=new_part):
            t, g = group_of(xp)
            shift = lax.rem(251 - 16 * g, LANES)
            sigma = W[3, xp]
            inside = (row_mask * x_mask(xp)) > 0.0
            fluxes = []
            for f in range(4):
                end = roll(UD[f, t], shift, 1)
                d = ND[f, xp]
                wx = sigma * (ND[f, xp + 1] - d)
                wy = sigma * (up_row(d) - d)
                wz = sigma * (jnp.where(lane == LANES - 1, end, up_lane(d)) - d)
                applied = (
                    (carry[f] - wx) + (down_row(wy) - wy)
                    + (jnp.where(lane == 0, end, down_lane(wz)) - wz)
                )
                if f > 0:
                    applied = applied + sigma * d
                res = NR[f, xp] - applied
                NR[f, xp] = res
                new = jnp.where(inside, keep_part * d + new_part * res, 0.0)
                ND[f, xp] = new
                NY[f, xp] = NY[f, xp] + new
                fluxes.append(wx)
            return tuple(fluxes)

        low, high = n + 1, B - n
        begin = tuple(W[3, low - 1] * (ND[f, low] - ND[f, low - 1]) for f in range(4))
        lax.fori_loop(low, high, node_body, begin)

    @pl.loop(0, N)
    def _(x):
        xp = x + H
        t, g = group_of(xp)
        shift = lax.rem(251 - 16 * g, LANES)
        potential = NY[0, xp]
        last_lane = lane == LANES - 1
        pieces = (
            (NY[0, xp + 1], NY[1, xp], NY[1, xp + 1]),
            (up_row(potential), NY[2, xp], up_row(NY[2, xp])),
            (
                jnp.where(last_lane, roll(PY[0, t], shift, 1), up_lane(potential)),
                NY[3, xp],
                jnp.where(last_lane, roll(PY[3, t], shift, 1), up_lane(NY[3, xp])),
            ),
        )
        for c, (above, own_part, next_part) in enumerate(pieces):
            out[c, x] = ((above - potential) + 0.5 * (own_part + next_part))[OWN]

    for copy in copies:
        copy.wait()

    @pl.loop(0, B)
    def _(xp):
        inside = (row_mask * x_mask(xp)) > 0.0
        for c in range(3):
            E2[c, xp] = jnp.where(inside, E2[c, xp], 0.0)

    assemble(E2, QRE, PE2, 3)
    for colour in range(4):
        turn(colour, E2, PE2, 3 - colour)

    @pl.loop(0, N)
    def _(x):
        for c in range(3):
            out[c, x] = out[c, x] + E2[c, x + H, OWN]


def solution(mesh):
    sizes = tuple(mesh.shape[a] for a in AXES)

    def on_device(right_side, labels, colors, table):
        f32 = jnp.float32
        plain = lambda n: pltpu.VMEM((n, B, B, LANES), f32)
        packed = lambda n: pltpu.VMEM((n, 3, B, LANES), f32)
        any_spec = pl.BlockSpec(memory_space=pl.ANY)
        return pl.pallas_call(
            functools.partial(kernel, sizes),
            out_shape=jax.ShapeDtypeStruct(right_side.shape, f32),
            in_specs=[any_spec, any_spec, any_spec, pl.BlockSpec(memory_space=pltpu.SMEM)],
            out_specs=pl.BlockSpec(memory_space=pltpu.VMEM),
            scratch_shapes=[
                pltpu.VMEM((3, N, N, LANES), f32),
                pltpu.VMEM((N, N, LANES), jnp.int32),
                pltpu.VMEM((3, N, N, LANES), jnp.int32),
                plain(7),
                pltpu.VMEM((7, 2, B, LANES), f32),
                pltpu.VMEM((2, 7, 4, B, LANES), f32),
                packed(7),
                pltpu.VMEM((B, B, LANES), f32),
                pltpu.VMEM((3, B, LANES), f32),
                pltpu.VMEM((3, B, LANES), f32),
                pltpu.VMEM((3, B, LANES), f32),
                plain(3),
                packed(3),
                plain(3),
                packed(3),
                pltpu.VMEM((3, 2, B, LANES), f32),
                pltpu.VMEM((2, 3, 4, B, LANES), f32),
                packed(2),
                plain(4),
                plain(4),
                plain(4),
                packed(4),
                packed(4),
                packed(4),
                packed(4),
                pltpu.SemaphoreType.DMA((3,)),
                pltpu.SemaphoreType.DMA((2, len(DIRS))),
                pltpu.SemaphoreType.DMA((2, len(DIRS))),
            ],
            compiler_params=pltpu.CompilerParams(
                collective_id=0, has_side_effects=True, vmem_limit_bytes=40 * 1024 * 1024
            ),
            cost_estimate=pl.CostEstimate(flops=10**8, bytes_accessed=2 * 10**6, transcendentals=0),
        )(right_side, labels, colors, table)

    in_specs = (P(None, "gx", "gy", "gz"), P("gx", "gy", "gz"), P(None, "gx", "gy", "gz"), P())
    return jax.shard_map(
        on_device, mesh=mesh, in_specs=in_specs, out_specs=P(None, "gx", "gy", "gz"), check_vma=False
    )
```

profile of v0, /device:TPU:1, one launch (start us, length us, event | category | flops | bytes accessed | tf_op | source)
XLA Modules:
  0.0 75.5 jit_solution(31485263478587860)
XLA Ops:
  0.0 0.0 copy-start
  0.0 1.0 %copy-done = f32[3,16,16,128]{3,2,1,0:T(8,128)S(1)} copy-done((f32[3,16,16,128]{3,2,1,0:T(8,128)S(1)}, f32[3,16,16,128]{3,2,1,0:T(8,128)}, u32[]{:S(2)}) %copy-start) | copy-done | bytes 393240
  1.0 0.0 copy-start.1
  1.0 1.0 %copy-done.1 = s32[3,16,16,128]{3,2,1,0:T(8,128)S(1)} copy-done((s32[3,16,16,128]{3,2,1,0:T(8,128)S(1)}, s32[3,16,16,128]{3,2,1,0:T(8,128)}, u32[]{:S(2)}) %copy-start.1) | copy-done | bytes 393240
  2.0 0.0 copy-start.2
  2.0 0.9 %copy-done.2 = s32[16,16,128]{2,1,0:T(8,128)S(1)} copy-done((s32[16,16,128]{2,1,0:T(8,128)S(1)}, s32[16,16,128]{2,1,0:T(8,128)}, u32[]{:S(2)}) %copy-start.2) | copy-done | bytes 131096
  2.9 0.0 copy-start.3
  2.9 0.7 copy-done.3
  3.6 71.1 %shard_map.46 = f32[3,16,16,128]{3,2,1,0:T(8,128)S(1)} custom-call(f32[3,16,16,128]{3,2,1,0:T(8,128)S(1)} %copy-done, s32[16,16,128]{2,1,0:T(8,128)S(1)} %copy-done.2, s32[3,16,16,128]{3,2,1,0:T(8,128)S(1)} %copy-done.1, f32[16]{0:T(128)S(1)} %copy-done.3), custom_call_target="tpu_custom_call" | custom-call | flops 100000000 | bytes 2000000 | tf_op jit(solution)/shard_map/pallas_call | solution.py:424
  74.7 0.7 copy.6
Async XLA Ops:
  0.0 1.0 %copy-start = (f32[3,16,16,128]{3,2,1,0:T(8,128)S(1)}, f32[3,16,16,128]{3,2,1,0:T(8,128)}, u32[]{:S(2)}) copy-start(f32[3,16,16,128]{3,2,1,0:T(8,128)} %r_hbm.1) | copy-start | bytes 1179652
  1.0 1.0 %copy-start.1 = (s32[3,16,16,128]{3,2,1,0:T(8,128)S(1)}, s32[3,16,16,128]{3,2,1,0:T(8,128)}, u32[]{:S(2)}) copy-start(s32[3,16,16,128]{3,2,1,0:T(8,128)} %col_hbm.1) | copy-start | bytes 1179652
  2.0 0.9 %copy-start.2 = (s32[16,16,128]{2,1,0:T(8,128)S(1)}, s32[16,16,128]{2,1,0:T(8,128)}, u32[]{:S(2)}) copy-start(s32[16,16,128]{2,1,0:T(8,128)} %lab_hbm.1) | copy-start | bytes 393220
  2.9 0.7 copy-start.3
where the time goes:
time: 75.7 us; the launch traced here: 75.5 us
  Pallas kernels  71.1 us (94%)
  local copies, waits for them, and re-layouts  4.3 us (6%)
    pallas_call x1, Pallas kernels, on_device(): pl.pallas_call(functools.partial(kernel, sizes), out_shape=jax.ShapeDtype...  71.1 us
    unnamed x9, local copies, waits for them, and re-layouts  4.3 us

commit v1 on v0

--- a/solution.py
+++ b/solution.py
@@ -17,6 +17,8 @@
 N = 16
 B = N + 2 * H
 LANES = 128
+BATCH = 5
+NBATCH = 7
 OWN = slice(H, H + N)
 DIRS = [d for d in itertools.product((-1, 0, 1), repeat=3) if d != (0, 0, 0)]
 
@@ -42,8 +44,8 @@
 
 
 def group_of(xp):
-    ring = lax.rem(xp + (B - H), B)
-    return ring // 8, lax.rem(ring, 8)
+    ring = (xp + (B - H)) % B if isinstance(xp, int) else jnp.where(xp >= H, xp - H, xp + (B - H))
+    return ring >> 3, ring & 7
 
 
 def select_table(labels, table):
@@ -65,9 +67,17 @@
     in_sem, ssem, rsem,
 ):
     here = [lax.axis_index(a) for a in AXES]
+    places = [
+        {
+            0: here[i],
+            1: jnp.where(here[i] == sizes[i] - 1, 0, here[i] + 1),
+            -1: jnp.where(here[i] == 0, sizes[i] - 1, here[i] - 1),
+        }
+        for i in range(3)
+    ]
 
     def neighbour(d):
-        return tuple(lax.rem(here[i] + (d[i] + sizes[i]), sizes[i]) for i in range(3))
+        return tuple(places[i][d[i]] for i in range(3))
 
     barrier = pltpu.get_barrier_semaphore()
     for d in DIRS:
@@ -97,9 +107,13 @@
         PMASK[t] = ends * before * after if t == 2 else ends
 
     def x_low(xp):
+        if isinstance(xp, int):
+            return first[0] if xp < H else 1.0
         return jnp.where(xp >= H, 1.0, first[0])
 
     def x_mask(xp):
+        if isinstance(xp, int):
+            return last[0] if xp >= H + N else x_low(xp)
         return x_low(xp) * jnp.where(xp < H + N, 1.0, last[0])
 
     for load in loads:
@@ -233,41 +247,61 @@
     def turn(colour, edges, packed, reach, target=None):
         packed_turn(colour, packed)
 
-        def faces(xp):
+        def ends_at(xp):
             t, g = group_of(xp)
-            shift = lax.rem(251 - 16 * g, LANES)
-            end_x, end_y = roll(U[0, t], shift, 1), roll(U[1, t], shift, 1)
+            shift = (251 - 16 * g) & (LANES - 1)
+            return roll(U[0, t], shift, 1), roll(U[1, t], shift, 1)
+
+        def moved(xp):
             ex, ey, ez = (edges[c, xp] for c in range(3))
-            ex_z = jnp.where(lane == LANES - 1, end_x, up_lane(ex))
-            ey_z = jnp.where(lane == LANES - 1, end_y, up_lane(ey))
+            return ex, ey, ez, edges[1, xp + 1], edges[2, xp + 1], up_lane(ex), up_lane(ey)
+
+        def faces(xp, values, fill):
+            ex, ey, ez, ey_x, ez_x, ex_z, ey_z = values
+            ex_z = jnp.where(lane == LANES - 1, fill[0], ex_z)
+            ey_z = jnp.where(lane == LANES - 1, fill[1], ey_z)
             keep = low_rows * x_low(xp)
             fx = (ey - ey_z + up_row(ez) - ez) * keep
-            fy = (ez - edges[2, xp + 1] + ex_z - ex) * keep
-            fz = (ex - up_row(ex) + edges[1, xp + 1] - ey) * keep
-            return fx, fy, fz, end_x, end_y, (ex, ey, ez)
-
-        def body(xp, carry):
+            fy = (ez - ez_x + ex_z - ex) * keep
+            fz = (ex - up_row(ex) + ey_x - ey) * keep
+            return fx, fy, fz
+
+        def planes_turn(planes, carry):
             fyp, fzp = carry
-            fx, fy, fz, end_x, end_y, old = faces(xp)
-            fx_z = jnp.where(lane == 0, end_y, down_lane(fx))
-            fy_z = jnp.where(lane == 0, end_x, down_lane(fy))
-            back = (
-                fz - down_row(fz) - fy + fy_z,
-                fx - fx_z - fz + fzp,
-                fy - fyp - fx + down_row(fx),
-            )
-            sigma, inverse = W[3, xp], INV[xp]
-            for c in range(3):
-                residual = W[c, xp] - back[c] - sigma * old[c]
-                value = old[c] + jnp.where(W[4 + c, xp] == colour + 1.0, residual * inverse, 0.0)
-                if target is None:
-                    edges[c, xp] = value
-                else:
-                    target[c, xp, OWN] = value[OWN]
-            return fy, fz
-
-        start = faces(H - reach - 1)
-        lax.fori_loop(H - reach, H + N + reach, body, (start[1], start[2]))
+            fills = [ends_at(xp) for xp in planes]
+            olds = [moved(xp) for xp in planes]
+            fs = [faces(xp, old, fill) for xp, old, fill in zip(planes, olds, fills)]
+            backs = [(down_lane(f[0]), down_lane(f[1])) for f in fs]
+            values = []
+            for xp, old, fill, (fx, fy, fz), (fx_z, fy_z) in zip(planes, olds, fills, fs, backs):
+                fx_z = jnp.where(lane == 0, fill[1], fx_z)
+                fy_z = jnp.where(lane == 0, fill[0], fy_z)
+                back = (
+                    fz - down_row(fz) - fy + fy_z,
+                    fx - fx_z - fz + fzp,
+                    fy - fyp - fx + down_row(fx),
+                )
+                fyp, fzp = fy, fz
+                sigma, inverse = W[3, xp], INV[xp]
+                for c in range(3):
+                    residual = W[c, xp] - back[c] - sigma * old[c]
+                    values.append(
+                        old[c] + jnp.where(W[4 + c, xp] == colour + 1.0, residual * inverse, 0.0)
+                    )
+            for i, xp in enumerate(planes):
+                for c in range(3):
+                    if target is None:
+                        edges[c, xp] = values[3 * i + c]
+                    else:
+                        target[c, xp, OWN] = values[3 * i + c][OWN]
+            return fyp, fzp
+
+        begin = H - reach - 1
+        start = faces(begin, moved(begin), ends_at(begin))
+        carry = (start[1], start[2])
+        every = list(range(H - reach, H + N + reach))
+        for i in range(0, len(every), BATCH):
+            carry = planes_turn(every[i : i + BATCH], carry)
 
     turn(1, E, PE, 2)
     turn(2, E, PE, 1)
@@ -287,7 +321,7 @@
     @pl.loop(1, B)
     def _(xp):
         t, g = group_of(xp)
-        end = roll(PW[2, t], lax.rem(245 - 16 * g, LANES), 1)
+        end = roll(PW[2, t], (245 - 16 * g) & (LANES - 1), 1)
         inside = (row_mask * x_mask(xp)) > 0.0
         own = [W[c, xp] for c in range(3)]
         below = [W[0, xp - 1], down_row(own[1]), jnp.where(lane == 0, end, down_lane(own[2]))]
@@ -345,41 +379,47 @@
                 PD[f, t] = new
                 PY[f, t] = PY[f, t] + new
 
-        def node_body(xp, carry, keep_part=keep_part, new_part=new_part):
-            t, g = group_of(xp)
-            shift = lax.rem(251 - 16 * g, LANES)
-            sigma = W[3, xp]
-            inside = (row_mask * x_mask(xp)) > 0.0
-            fluxes = []
-            for f in range(4):
-                end = roll(UD[f, t], shift, 1)
-                d = ND[f, xp]
-                wx = sigma * (ND[f, xp + 1] - d)
-                wy = sigma * (up_row(d) - d)
-                wz = sigma * (jnp.where(lane == LANES - 1, end, up_lane(d)) - d)
-                applied = (
-                    (carry[f] - wx) + (down_row(wy) - wy)
-                    + (jnp.where(lane == 0, end, down_lane(wz)) - wz)
-                )
-                if f > 0:
-                    applied = applied + sigma * d
-                res = NR[f, xp] - applied
-                NR[f, xp] = res
-                new = jnp.where(inside, keep_part * d + new_part * res, 0.0)
-                ND[f, xp] = new
-                NY[f, xp] = NY[f, xp] + new
-                fluxes.append(wx)
-            return tuple(fluxes)
-
         low, high = n + 1, B - n
-        begin = tuple(W[3, low - 1] * (ND[f, low] - ND[f, low - 1]) for f in range(4))
-        lax.fori_loop(low, high, node_body, begin)
+
+        @pl.loop(0, 4)
+        def _(f, keep_part=keep_part, new_part=new_part, low=low, high=high):
+            mass = jnp.where(f > 0, 1.0, 0.0)
+            wxp = W[3, low - 1] * (ND[f, low] - ND[f, low - 1])
+            for i in range(low, high, NBATCH):
+                planes = list(range(i, min(i + NBATCH, high)))
+                ends = []
+                for xp in planes:
+                    t, g = group_of(xp)
+                    ends.append(roll(UD[f, t], (251 - 16 * g) % LANES, 1))
+                ds = [ND[f, xp] for xp in planes] + [ND[f, planes[-1] + 1]]
+                ups = [up_lane(d) for d in ds[:-1]]
+                sigmas = [W[3, xp] for xp in planes]
+                wzs = [
+                    sigma * (jnp.where(lane == LANES - 1, end, up) - d)
+                    for sigma, end, up, d in zip(sigmas, ends, ups, ds)
+                ]
+                downs = [down_lane(wz) for wz in wzs]
+                for j, xp in enumerate(planes):
+                    d, sigma, wz = ds[j], sigmas[j], wzs[j]
+                    wx = sigma * (ds[j + 1] - d)
+                    wy = sigma * (up_row(d) - d)
+                    applied = (
+                        (mass * sigma) * d + (wxp - wx) + (down_row(wy) - wy)
+                        + (jnp.where(lane == 0, ends[j], downs[j]) - wz)
+                    )
+                    wxp = wx
+                    res = NR[f, xp] - applied
+                    inside = (row_mask * x_mask(xp)) > 0.0
+                    new = jnp.where(inside, keep_part * d + new_part * res, 0.0)
+                    NR[f, xp] = res
+                    ND[f, xp] = new
+                    NY[f, xp] = NY[f, xp] + new
 
     @pl.loop(0, N)
     def _(x):
         xp = x + H
         t, g = group_of(xp)
-        shift = lax.rem(251 - 16 * g, LANES)
+        shift = (251 - 16 * g) & (LANES - 1)
         potential = NY[0, xp]
         last_lane = lane == LANES - 1
         pieces = (

time: 75.7 us -> 51.9 us (0.69)
  Pallas kernels: 71.1 us -> 47.4 us
    pallas_call x1, Pallas kernels: 71.1 us -> 47.4 us  [on_device(): pl.pallas_call(functools.partial(kernel, sizes), out_shape=jax.ShapeDtype...]
where the time goes in v1:
time: 51.9 us; the launch traced here: 51.7 us
  Pallas kernels  47.4 us (91%)
  local copies, waits for them, and re-layouts  4.3 us (8%)
    pallas_call x1, Pallas kernels, on_device(): pl.pallas_call(functools.partial(kernel, sizes), out_shape=jax.ShapeDtype...  47.4 us
    unnamed x9, local copies, waits for them, and re-layouts  4.3 us

profile of v1, /device:TPU:1, one launch (start us, length us, event | category | flops | bytes accessed | tf_op | source)
XLA Modules:
  0.0 51.7 jit_solution(1566734083872067146)
XLA Ops:
  0.0 0.0 copy-start
  0.0 1.0 %copy-done = f32[3,16,16,128]{3,2,1,0:T(8,128)S(1)} copy-done((f32[3,16,16,128]{3,2,1,0:T(8,128)S(1)}, f32[3,16,16,128]{3,2,1,0:T(8,128)}, u32[]{:S(2)}) %copy-start) | copy-done | bytes 393240
  1.0 0.0 copy-start.1
  1.0 1.0 %copy-done.1 = s32[3,16,16,128]{3,2,1,0:T(8,128)S(1)} copy-done((s32[3,16,16,128]{3,2,1,0:T(8,128)S(1)}, s32[3,16,16,128]{3,2,1,0:T(8,128)}, u32[]{:S(2)}) %copy-start.1) | copy-done | bytes 393240
  2.0 0.0 copy-start.2
  2.0 0.9 %copy-done.2 = s32[16,16,128]{2,1,0:T(8,128)S(1)} copy-done((s32[16,16,128]{2,1,0:T(8,128)S(1)}, s32[16,16,128]{2,1,0:T(8,128)}, u32[]{:S(2)}) %copy-start.2) | copy-done | bytes 131096
  2.9 0.0 copy-start.3
  2.9 0.7 %copy-done.3 = f32[16]{0:T(128)S(1)} copy-done((f32[16]{0:T(128)S(1)}, f32[16]{0:T(128)}, u32[]{:S(2)}) %copy-start.3) | copy-done | bytes 88
  3.6 47.4 %shard_map.46 = f32[3,16,16,128]{3,2,1,0:T(8,128)S(1)} custom-call(f32[3,16,16,128]{3,2,1,0:T(8,128)S(1)} %copy-done, s32[16,16,128]{2,1,0:T(8,128)S(1)} %copy-done.2, s32[3,16,16,128]{3,2,1,0:T(8,128)S(1)} %copy-done.1, f32[16]{0:T(128)S(1)} %copy-done.3), custom_call_target="tpu_custom_call" | custom-call | flops 100000000 | bytes 2000000 | tf_op jit(solution)/shard_map/pallas_call | solution.py:464
  51.0 0.7 %copy.6 = f32[3,16,16,128]{3,2,1,0:T(8,128)} copy(f32[3,16,16,128]{3,2,1,0:T(8,128)S(1)} %shard_map.46) | data formatting | bytes 786432
Async XLA Ops:
  0.0 1.0 %copy-start = (f32[3,16,16,128]{3,2,1,0:T(8,128)S(1)}, f32[3,16,16,128]{3,2,1,0:T(8,128)}, u32[]{:S(2)}) copy-start(f32[3,16,16,128]{3,2,1,0:T(8,128)} %r_hbm.1) | copy-start | bytes 1179652
  1.0 1.0 %copy-start.1 = (s32[3,16,16,128]{3,2,1,0:T(8,128)S(1)}, s32[3,16,16,128]{3,2,1,0:T(8,128)}, u32[]{:S(2)}) copy-start(s32[3,16,16,128]{3,2,1,0:T(8,128)} %col_hbm.1) | copy-start | bytes 1179652
  2.0 0.9 %copy-start.2 = (s32[16,16,128]{2,1,0:T(8,128)S(1)}, s32[16,16,128]{2,1,0:T(8,128)}, u32[]{:S(2)}) copy-start(s32[16,16,128]{2,1,0:T(8,128)} %lab_hbm.1) | copy-start | bytes 393220
  2.9 0.7 %copy-start.3 = (f32[16]{0:T(128)S(1)}, f32[16]{0:T(128)}, u32[]{:S(2)}) copy-start(f32[16]{0:T(128)} %tab.1) | copy-start | bytes 196

commit v2 on v1

--- a/solution.py
+++ b/solution.py
@@ -20,7 +20,8 @@
 BATCH = 5
 NBATCH = 7
 OWN = slice(H, H + N)
-DIRS = [d for d in itertools.product((-1, 0, 1), repeat=3) if d != (0, 0, 0)]
+DIRS = [d for d in itertools.product((-1, 0, 1), repeat=3) if 0 < sum(map(abs, d)) < 3]
+RELAYS = [(dx, dy) for dx in (-1, 1) for dy in (-1, 1)]
 
 
 def roll(values, shift, axis):
@@ -58,14 +59,16 @@
 
 def kernel(
     sizes,
-    r_hbm, lab_hbm, col_hbm, tab,
+    r_hbm, lab_hbm, col_hbm, tab_hbm,
     out,
-    r_in, lab_in, col_in,
+    r_in, lab_in, col_in, tab,
     W, QM, QR, PW, INV, PINV, PMASK, PKEEP,
     E, PE, E2, PE2, QME, QRE, U,
     NR, ND, NY, PR, PD, PY, UD,
+    xs_w, xr_w, xp_w, xc_w, xs_e, xr_e, xp_e, xc_e,
     in_sem, ssem, rsem,
 ):
+    XW, XE = (xs_w, xr_w, xp_w, xc_w), (xs_e, xr_e, xp_e, xc_e)
     here = [lax.axis_index(a) for a in AXES]
     places = [
         {
@@ -79,15 +82,36 @@
     def neighbour(d):
         return tuple(places[i][d[i]] for i in range(3))
 
-    barrier = pltpu.get_barrier_semaphore()
-    for d in DIRS:
-        pl.semaphore_signal(barrier, inc=1, device_id=neighbour(d), device_id_type=pl.DeviceIdType.MESH)
+    def exists(d):
+        found = None
+        for i in range(3):
+            if d[i]:
+                one = here[i] < sizes[i] - 1 if d[i] > 0 else here[i] > 0
+                found = one if found is None else jnp.logical_and(found, one)
+        return found
+
+    def opposite(d):
+        return tuple(-step for step in d)
+
     loads = [
         pltpu.make_async_copy(src, dst, in_sem.at[i])
-        for i, (src, dst) in enumerate(((lab_hbm, lab_in), (r_hbm, r_in), (col_hbm, col_in)))
+        for i, (src, dst) in enumerate(
+            ((tab_hbm, tab), (lab_hbm, lab_in), (r_hbm, r_in), (col_hbm, col_in))
+        )
     ]
     for load in loads:
         load.start()
+    barrier = pltpu.get_barrier_semaphore()
+    around = jnp.int32(0)
+    for d in DIRS:
+        around = around + exists(d).astype(jnp.int32)
+
+        @pl.when(exists(d))
+        def _(d=d):
+            pl.semaphore_signal(
+                barrier, inc=1, device_id=neighbour(d), device_id_type=pl.DeviceIdType.MESH
+            )
+
 
     first = [jnp.where(here[i] > 0, 1.0, 0.0).astype(jnp.float32) for i in range(3)]
     last = [jnp.where(here[i] < sizes[i] - 1, 1.0, 0.0).astype(jnp.float32) for i in range(3)]
@@ -119,7 +143,7 @@
     for load in loads:
         load.wait()
 
-    @pl.loop(0, N)
+    @pl.loop(0, N, unroll=4)
     def _(x):
         W[3, x + H, OWN] = select_table(lab_in[x], tab)
         for c in range(3):
@@ -139,7 +163,7 @@
                 dst[f, t, OWN] = total
 
     pack_own(W, QM, 7)
-    pl.semaphore_wait(barrier, len(DIRS))
+    pl.semaphore_wait(barrier, around)
 
     def span(d, side):
         if d == 0:
@@ -149,36 +173,91 @@
             return slice(0, H) if low else slice(H + N, B)
         return slice(H, 2 * H) if d < 0 else slice(N, N + H)
 
-    def exchange(phase, main, packed, received):
-        copies = []
+    def merge(parts, half):
+        shape = parts[0].shape
+        lanes = lax.broadcasted_iota(jnp.int32, shape, 1)
+        pair = lanes % 16 < 8
+        out = jnp.where(pair, parts[0], roll(parts[1], 8, 1))
+        other = roll(parts[2], 64, 1)
+        if len(parts) > 3:
+            other = jnp.where(pair, other, roll(parts[3], 72, 1))
+        return jnp.where((lanes < 64) == (half == 0), out, other)
+
+    def groups(fields):
+        return [list(range(i, min(i + 4, fields))) for i in range(0, fields, 4)]
+
+    def remote(phase, i, src, dst, d):
+        return pltpu.make_async_remote_copy(
+            src_ref=src,
+            dst_ref=dst,
+            send_sem=ssem.at[phase, i],
+            recv_sem=rsem.at[phase, i],
+            device_id=neighbour(d),
+            device_id_type=pl.DeviceIdType.MESH,
+        )
+
+    def exchange(phase, main, packed, received, sides, fields):
+        sent, got = sides[0], sides[1]
+        tiles = len(groups(fields))
+        for h in range(2):
+            for k, group in enumerate(groups(fields)):
+                sent[h, k] = merge([packed[f, h, OWN] for f in group], h)
+        copies = {}
         for i, d in enumerate(DIRS):
             rows_src, rows_dst = span(d[1], "src"), span(d[1], "dst")
             if d[2] == 0:
                 src = main.at[:, span(d[0], "src"), rows_src]
                 dst = main.at[:, span(d[0], "dst"), rows_dst]
+            elif d[0] == 0:
+                src = packed.at[:, :, rows_src]
+                dst = received.at[1 if d[2] > 0 else 0, :, :, rows_dst]
             else:
-                slot_src = {0: slice(0, 2), 1: slice(1, 2), -1: slice(0, 1)}[d[0]]
-                slot_dst = {0: slice(0, 2), 1: slice(3, 4), -1: slice(2, 3)}[d[0]]
-                src = packed.at[:, slot_src, rows_src]
-                dst = received.at[1 if d[2] > 0 else 0, :, slot_dst, rows_dst]
-            copies.append(
-                pltpu.make_async_remote_copy(
-                    src_ref=src,
-                    dst_ref=dst,
-                    send_sem=ssem.at[phase, i],
-                    recv_sem=rsem.at[phase, i],
-                    device_id=neighbour(d),
-                    device_id_type=pl.DeviceIdType.MESH,
-                )
+                h = 1 if d[0] > 0 else 0
+                src = sent.at[h]
+                dst = got.at[1 if d[2] > 0 else 0, h, :, rows_dst]
+            copies[d] = remote(phase, i, src, dst, d)
+        rank = lambda d: (abs(d[1]) * abs(d[2]) == 0, abs(d[0]) * abs(d[2]) == 0, -abs(d[0]), -abs(d[2]))
+        for d in sorted(DIRS, key=rank):
+            pl.when(exists(d))(copies[d].start)
+        return copies
+
+    def relay(phase, copies, received, sides, fields):
+        passed, corner = sides[2], sides[3]
+        for d in DIRS:
+            if d[0] == 0 and d[1] and d[2]:
+                pl.when(exists(opposite(d)))(copies[d].wait_recv)
+        narrow = lax.broadcasted_iota(jnp.int32, (H, LANES), 1) % 16 < 4
+        for i, (dx, dy) in enumerate(RELAYS):
+            h, rows = (1 if dx > 0 else 0), (slice(0, H) if dy < 0 else slice(H + N, B))
+            for k, group in enumerate(groups(fields)):
+                parts = [jnp.where(narrow, received[1, f, h, rows], received[0, f, h, rows]) for f in group]
+                passed[i, k, 0:H] = merge(parts, h)
+            copy = remote(
+                phase, len(DIRS) + i, passed.at[i, :, 0:H], corner.at[h, :, rows], (dx, 0, 0)
             )
-        order = sorted(range(len(DIRS)), key=lambda i: (-abs(DIRS[i][0]), sum(map(abs, DIRS[i]))))
-        for i in order:
-            copies[i].start()
-        return copies
-
-    def assemble(src, received, dst, fields):
-        @pl.loop(0, fields)
-        def _(f):
+            pl.when(exists((dx, 0, 0)))(copy.start)
+            copies[(dx, dy)] = copy
+
+    def finish(copies):
+        for d, copy in copies.items():
+            way = d if len(d) == 3 else (d[0], 0, 0)
+            if len(d) == 2 or d[0] or not (d[1] and d[2]):
+                pl.when(exists(opposite(way)))(copy.wait_recv)
+            pl.when(exists(way))(copy.wait_send)
+
+    def assemble(src, received, sides, dst, fields):
+        got, corner = sides[1], sides[3]
+        edge_rows = (row < H) | (row >= H + N)
+        left = lane < 64
+        across = [[None] * fields, [None] * fields]
+        for side in range(2):
+            for k, group in enumerate(groups(fields)):
+                high, low = (jnp.where(edge_rows, corner[h, k], got[side, h, k]) for h in range(2))
+                near, far = jnp.where(left, high, low), jnp.where(left, low, high)
+                moved = (near, roll(near, 120, 1), roll(far, 64, 1), roll(far, 56, 1))
+                for f, value in zip(group, moved):
+                    across[side][f] = value
+        for f in range(fields):
             for t in range(3):
                 own = None
                 for g in range(8):
@@ -188,17 +267,16 @@
                 if t < 2:
                     high, low = received[0, f, t], received[1, f, t]
                 else:
-                    high = jnp.where(lane < 64, received[0, f, 2], received[0, f, 3])
-                    low = jnp.where(lane < 64, received[1, f, 2], received[1, f, 3])
+                    high, low = across[0][f], across[1][f]
                 upper = jnp.where(spot < 4, own, high)
                 lower = roll(jnp.where(spot < 4, low, own), 8, 1)
                 dst[f, t] = jnp.where(PMASK[t] > 0.0, jnp.where(spot < 8, upper, lower), 0.0)
 
-    copies = exchange(0, W, QM, QR)
-    for copy in copies:
-        copy.wait()
-
-    @pl.loop(0, B)
+    copies = exchange(0, W, QM, QR, XW, 7)
+    relay(0, copies, QR, XW, 7)
+    finish(copies)
+
+    @pl.loop(0, B, unroll=4)
     def _(xp):
         inside = (row_mask * x_mask(xp)) > 0.0
         for f in range(7):
@@ -208,7 +286,7 @@
         for c in range(3):
             E[c, xp] = jnp.where(W[4 + c, xp] == 1.0, W[c, xp] * inverse, 0.0)
 
-    assemble(W, QR, PW, 7)
+    assemble(W, QR, XW, PW, 7)
     for t in range(3):
         PINV[t] = 1.0 / (16.0 + PW[3, t])
         for c in range(3):
@@ -308,7 +386,7 @@
     turn(3, E, PE, 0, target=E2)
 
     pack_own(E2, QME, 3)
-    copies = exchange(1, E2, QME, QRE)
+    copies = exchange(1, E2, QME, QRE, XE, 3)
 
     top = tab[0]
     for i in range(1, 16):
@@ -318,7 +396,7 @@
     per_centre = (60.0 / 31.0) / upper
     per_half = (60.0 / 29.0) / upper
 
-    @pl.loop(1, B)
+    @pl.loop(1, B, unroll=6)
     def _(xp):
         t, g = group_of(xp)
         end = roll(PW[2, t], (245 - 16 * g) & (LANES - 1), 1)
@@ -415,7 +493,10 @@
                     ND[f, xp] = new
                     NY[f, xp] = NY[f, xp] + new
 
-    @pl.loop(0, N)
+        if n == 1:
+            relay(1, copies, QRE, XE, 3)
+
+    @pl.loop(0, N, unroll=4)
     def _(x):
         xp = x + H
         t, g = group_of(xp)
@@ -434,20 +515,19 @@
         for c, (above, own_part, next_part) in enumerate(pieces):
             out[c, x] = ((above - potential) + 0.5 * (own_part + next_part))[OWN]
 
-    for copy in copies:
-        copy.wait()
-
-    @pl.loop(0, B)
+    finish(copies)
+
+    @pl.loop(0, B, unroll=4)
     def _(xp):
         inside = (row_mask * x_mask(xp)) > 0.0
         for c in range(3):
             E2[c, xp] = jnp.where(inside, E2[c, xp], 0.0)
 
-    assemble(E2, QRE, PE2, 3)
+    assemble(E2, QRE, XE, PE2, 3)
     for colour in range(4):
         turn(colour, E2, PE2, 3 - colour)
 
-    @pl.loop(0, N)
+    @pl.loop(0, N, unroll=4)
     def _(x):
         for c in range(3):
             out[c, x] = out[c, x] + E2[c, x + H, OWN]
@@ -460,19 +540,26 @@
         f32 = jnp.float32
         plain = lambda n: pltpu.VMEM((n, B, B, LANES), f32)
         packed = lambda n: pltpu.VMEM((n, 3, B, LANES), f32)
-        any_spec = pl.BlockSpec(memory_space=pl.ANY)
+        across = lambda k: [
+            pltpu.VMEM((2, k, N, LANES), f32),
+            pltpu.VMEM((2, 2, k, B, LANES), f32),
+            pltpu.VMEM((len(RELAYS), k, 8, LANES), f32),
+            pltpu.VMEM((2, k, B, LANES), f32),
+        ]
+        any_spec = pl.BlockSpec(memory_space=pltpu.HBM)
         return pl.pallas_call(
             functools.partial(kernel, sizes),
             out_shape=jax.ShapeDtypeStruct(right_side.shape, f32),
-            in_specs=[any_spec, any_spec, any_spec, pl.BlockSpec(memory_space=pltpu.SMEM)],
+            in_specs=[any_spec] * 4,
             out_specs=pl.BlockSpec(memory_space=pltpu.VMEM),
             scratch_shapes=[
                 pltpu.VMEM((3, N, N, LANES), f32),
                 pltpu.VMEM((N, N, LANES), jnp.int32),
                 pltpu.VMEM((3, N, N, LANES), jnp.int32),
+                pltpu.SMEM((16,), f32),
                 plain(7),
                 pltpu.VMEM((7, 2, B, LANES), f32),
-                pltpu.VMEM((2, 7, 4, B, LANES), f32),
+                pltpu.VMEM((2, 7, 2, B, LANES), f32),
                 packed(7),
                 pltpu.VMEM((B, B, LANES), f32),
                 pltpu.VMEM((3, B, LANES), f32),
@@ -483,7 +570,7 @@
                 plain(3),
                 packed(3),
                 pltpu.VMEM((3, 2, B, LANES), f32),
-                pltpu.VMEM((2, 3, 4, B, LANES), f32),
+                pltpu.VMEM((2, 3, 2, B, LANES), f32),
                 packed(2),
                 plain(4),
                 plain(4),
@@ -492,12 +579,14 @@
                 packed(4),
                 packed(4),
                 packed(4),
-                pltpu.SemaphoreType.DMA((3,)),
-                pltpu.SemaphoreType.DMA((2, len(DIRS))),
-                pltpu.SemaphoreType.DMA((2, len(DIRS))),
+                *across(2),
+                *across(1),
+                pltpu.SemaphoreType.DMA((4,)),
+                pltpu.SemaphoreType.DMA((2, len(DIRS) + len(RELAYS))),
+                pltpu.SemaphoreType.DMA((2, len(DIRS) + len(RELAYS))),
             ],
             compiler_params=pltpu.CompilerParams(
-                collective_id=0, has_side_effects=True, vmem_limit_bytes=40 * 1024 * 1024
+                collective_id=0, has_side_effects=True, vmem_limit_bytes=63 * 1024 * 1024
             ),
             cost_estimate=pl.CostEstimate(flops=10**8, bytes_accessed=2 * 10**6, transcendentals=0),
         )(right_side, labels, colors, table)

time: 51.9 us -> 37.6 us (0.72)
  Pallas kernels: 47.4 us -> 35.6 us
  local copies, waits for them, and re-layouts: 4.3 us -> 1.77 us
    pallas_call x1, Pallas kernels: 47.4 us -> 35.6 us  [on_device(): pl.pallas_call(functools.partial(kernel, sizes), out_shape=jax.ShapeDtype...]
    unnamed x9 -> x1, local copies, waits for them, and re-layouts: 4.3 us -> 1.77 us
where the time goes in v2:
time: 37.6 us; the launch traced here: 37.4 us
  Pallas kernels  35.6 us (95%)
  local copies, waits for them, and re-layouts  1.77 us (5%)
    pallas_call x1, Pallas kernels, on_device(): pl.pallas_call(functools.partial(kernel, sizes), out_shape=jax.ShapeDtype...  35.6 us
    unnamed x1, local copies, waits for them, and re-layouts  1.77 us

profile of v2, /device:TPU:1, one launch (start us, length us, event | category | flops | bytes accessed | tf_op | source)
XLA Modules:
  0.0 37.4 jit_solution(10473149836567768955)
XLA Ops:
  0.0 35.6 %shard_map.46 = f32[3,16,16,128]{3,2,1,0:T(8,128)} custom-call(f32[3,16,16,128]{3,2,1,0:T(8,128)} %r_hbm.1, s32[16,16,128]{2,1,0:T(8,128)} %lab_hbm.1, s32[3,16,16,128]{3,2,1,0:T(8,128)} %col_hbm.1, f32[16]{0:T(128)} %tab_hbm.1), custom_call_target="tpu_custom_call" | custom-call | flops 100000000 | bytes 2000000 | tf_op jit(solution)/shard_map/pallas_call | solution.py:550
  35.6 1.8 %copy.6 = f32[3,16,16,128]{3,2,1,0:T(8,128)} copy(f32[3,16,16,128]{3,2,1,0:T(8,128)} %shard_map.46) | data formatting | bytes 786432

commit v3 on v2

--- a/solution.py
+++ b/solution.py
@@ -65,10 +65,10 @@
     W, QM, QR, PW, INV, PINV, PMASK, PKEEP,
     E, PE, E2, PE2, QME, QRE, U,
     NR, ND, NY, PR, PD, PY, UD,
-    xs_w, xr_w, xp_w, xc_w, xs_e, xr_e, xp_e, xc_e,
+    xs_w, xr_w, xp_w, xc_w, zs_w, xs_e, xr_e, xp_e, xc_e, zs_e,
     in_sem, ssem, rsem,
 ):
-    XW, XE = (xs_w, xr_w, xp_w, xc_w), (xs_e, xr_e, xp_e, xc_e)
+    XW, XE = (xs_w, xr_w, xp_w, xc_w, zs_w), (xs_e, xr_e, xp_e, xc_e, zs_e)
     here = [lax.axis_index(a) for a in AXES]
     places = [
         {
@@ -163,7 +163,6 @@
                 dst[f, t, OWN] = total
 
     pack_own(W, QM, 7)
-    pl.semaphore_wait(barrier, around)
 
     def span(d, side):
         if d == 0:
@@ -183,6 +182,17 @@
             other = jnp.where(pair, other, roll(parts[3], 72, 1))
         return jnp.where((lanes < 64) == (half == 0), out, other)
 
+    def merge_quads(parts, base):
+        quad = lax.broadcasted_iota(jnp.int32, parts[0].shape, 1) % 16 // 4
+        out = parts[0]
+        for i, part in enumerate(parts[1:], 1):
+            out = jnp.where(quad == (base + i) % 4, roll(part, 4 * i, 1), out)
+        return out
+
+    def split_quad(received, side, f, t, rows):
+        value = received[side, f // 4, t, rows]
+        return value if f % 4 == 0 else roll(value, LANES - 4 * (f % 4), 1)
+
     def groups(fields):
         return [list(range(i, min(i + 4, fields))) for i in range(0, fields, 4)]
 
@@ -196,12 +206,16 @@
             device_id_type=pl.DeviceIdType.MESH,
         )
 
-    def exchange(phase, main, packed, received, sides, fields):
-        sent, got = sides[0], sides[1]
-        tiles = len(groups(fields))
+    def prepare(packed, sides, fields):
         for h in range(2):
             for k, group in enumerate(groups(fields)):
-                sent[h, k] = merge([packed[f, h, OWN] for f in group], h)
+                parts = [packed[f, h, OWN] for f in group]
+                sides[0][h, k] = merge(parts, h)
+                for side in range(2):
+                    sides[4][side, k, h] = merge_quads(parts, side)
+
+    def exchange(phase, main, received, sides):
+        sent, got = sides[0], sides[1]
         copies = {}
         for i, d in enumerate(DIRS):
             rows_src, rows_dst = span(d[1], "src"), span(d[1], "dst")
@@ -209,14 +223,15 @@
                 src = main.at[:, span(d[0], "src"), rows_src]
                 dst = main.at[:, span(d[0], "dst"), rows_dst]
             elif d[0] == 0:
-                src = packed.at[:, :, rows_src]
+                src = sides[4].at[0 if d[2] > 0 else 1, :, :, slice(rows_src.start - H, rows_src.stop - H)]
                 dst = received.at[1 if d[2] > 0 else 0, :, :, rows_dst]
             else:
                 h = 1 if d[0] > 0 else 0
                 src = sent.at[h]
                 dst = got.at[1 if d[2] > 0 else 0, h, :, rows_dst]
             copies[d] = remote(phase, i, src, dst, d)
-        rank = lambda d: (abs(d[1]) * abs(d[2]) == 0, abs(d[0]) * abs(d[2]) == 0, -abs(d[0]), -abs(d[2]))
+        turns = [(0, 1, 1), (1, 0, 1), (1, 1, 0), (0, 1, 0), (0, 0, 1), (1, 0, 0)]
+        rank = lambda d: turns.index(tuple(map(abs, d)))
         for d in sorted(DIRS, key=rank):
             pl.when(exists(d))(copies[d].start)
         return copies
@@ -230,7 +245,14 @@
         for i, (dx, dy) in enumerate(RELAYS):
             h, rows = (1 if dx > 0 else 0), (slice(0, H) if dy < 0 else slice(H + N, B))
             for k, group in enumerate(groups(fields)):
-                parts = [jnp.where(narrow, received[1, f, h, rows], received[0, f, h, rows]) for f in group]
+                parts = [
+                    jnp.where(
+                        narrow,
+                        split_quad(received, 1, f, h, rows),
+                        split_quad(received, 0, f, h, rows),
+                    )
+                    for f in group
+                ]
                 passed[i, k, 0:H] = merge(parts, h)
             copy = remote(
                 phase, len(DIRS) + i, passed.at[i, :, 0:H], corner.at[h, :, rows], (dx, 0, 0)
@@ -265,14 +287,16 @@
                     piece = roll(src[f, x], 16 * g + 4, 1)
                     own = piece if g == 0 else jnp.where(lane // 16 == g, piece, own)
                 if t < 2:
-                    high, low = received[0, f, t], received[1, f, t]
+                    high, low = (split_quad(received, side, f, t, slice(None)) for side in range(2))
                 else:
                     high, low = across[0][f], across[1][f]
                 upper = jnp.where(spot < 4, own, high)
                 lower = roll(jnp.where(spot < 4, low, own), 8, 1)
                 dst[f, t] = jnp.where(PMASK[t] > 0.0, jnp.where(spot < 8, upper, lower), 0.0)
 
-    copies = exchange(0, W, QM, QR, XW, 7)
+    prepare(QM, XW, 7)
+    pl.semaphore_wait(barrier, around)
+    copies = exchange(0, W, QR, XW)
     relay(0, copies, QR, XW, 7)
     finish(copies)
 
@@ -386,7 +410,8 @@
     turn(3, E, PE, 0, target=E2)
 
     pack_own(E2, QME, 3)
-    copies = exchange(1, E2, QME, QRE, XE, 3)
+    prepare(QME, XE, 3)
+    copies = exchange(1, E2, QRE, XE)
 
     top = tab[0]
     for i in range(1, 16):
@@ -435,7 +460,7 @@
         new_part = (2.0 * rho_next) * per_half
         rho = rho_next
 
-        @pl.loop(0, 4)
+        @pl.loop(0, 4, unroll=4)
         def _(f, keep_part=keep_part, new_part=new_part):
             mass = jnp.where(f > 0, 1.0, 0.0)
             d = [PD[f, t] for t in range(3)]
@@ -545,6 +570,7 @@
             pltpu.VMEM((2, 2, k, B, LANES), f32),
             pltpu.VMEM((len(RELAYS), k, 8, LANES), f32),
             pltpu.VMEM((2, k, B, LANES), f32),
+            pltpu.VMEM((2, k, 2, N, LANES), f32),
         ]
         any_spec = pl.BlockSpec(memory_space=pltpu.HBM)
         return pl.pallas_call(
@@ -559,7 +585,7 @@
                 pltpu.SMEM((16,), f32),
                 plain(7),
                 pltpu.VMEM((7, 2, B, LANES), f32),
-                pltpu.VMEM((2, 7, 2, B, LANES), f32),
+                pltpu.VMEM((2, 2, 2, B, LANES), f32),
                 packed(7),
                 pltpu.VMEM((B, B, LANES), f32),
                 pltpu.VMEM((3, B, LANES), f32),
@@ -570,7 +596,7 @@
                 plain(3),
                 packed(3),
                 pltpu.VMEM((3, 2, B, LANES), f32),
-                pltpu.VMEM((2, 3, 2, B, LANES), f32),
+                pltpu.VMEM((2, 1, 2, B, LANES), f32),
                 packed(2),
                 plain(4),
                 plain(4),

time: 37.6 us -> 36.8 us (0.979)
  Pallas kernels: 35.6 us -> 34.9 us
    pallas_call x1, Pallas kernels: 35.6 us -> 34.9 us  [on_device(): pl.pallas_call(functools.partial(kernel, sizes), out_shape=jax.ShapeDtype...]
where the time goes in v3:
time: 36.8 us; the launch traced here: 36.6 us
  Pallas kernels  34.9 us (95%)
  local copies, waits for them, and re-layouts  1.77 us (5%)
    pallas_call x1, Pallas kernels, on_device(): pl.pallas_call(functools.partial(kernel, sizes), out_shape=jax.ShapeDtype...  34.9 us
    unnamed x1, local copies, waits for them, and re-layouts  1.77 us

profile of v3, /device:TPU:1, one launch (start us, length us, event | category | flops | bytes accessed | tf_op | source)
XLA Modules:
  0.0 36.6 jit_solution(5188216944521272833)
XLA Ops:
  0.0 34.9 %shard_map.46 = f32[3,16,16,128]{3,2,1,0:T(8,128)} custom-call(f32[3,16,16,128]{3,2,1,0:T(8,128)} %r_hbm.1, s32[16,16,128]{2,1,0:T(8,128)} %lab_hbm.1, s32[3,16,16,128]{3,2,1,0:T(8,128)} %col_hbm.1, f32[16]{0:T(128)} %tab_hbm.1), custom_call_target="tpu_custom_call" | custom-call | flops 100000000 | bytes 2000000 | tf_op jit(solution)/shard_map/pallas_call | solution.py:576
  34.9 1.8 %copy.6 = f32[3,16,16,128]{3,2,1,0:T(8,128)} copy(f32[3,16,16,128]{3,2,1,0:T(8,128)} %shard_map.46) | data formatting | bytes 786432

commit v4 on v3

--- a/solution.py
+++ b/solution.py
@@ -164,13 +164,13 @@
 
     pack_own(W, QM, 7)
 
-    def span(d, side):
+    def span(d, side, depth=H):
         if d == 0:
             return slice(H, H + N)
         low = (d > 0) == (side == "dst")
         if side == "dst":
-            return slice(0, H) if low else slice(H + N, B)
-        return slice(H, 2 * H) if d < 0 else slice(N, N + H)
+            return slice(H - depth, H) if low else slice(H + N, H + N + depth)
+        return slice(H, H + depth) if d < 0 else slice(H + N - depth, H + N)
 
     def merge(parts, half):
         shape = parts[0].shape
@@ -220,8 +220,16 @@
         for i, d in enumerate(DIRS):
             rows_src, rows_dst = span(d[1], "src"), span(d[1], "dst")
             if d[2] == 0:
-                src = main.at[:, span(d[0], "src"), rows_src]
-                dst = main.at[:, span(d[0], "dst"), rows_dst]
+                src = main.at[0:3, span(d[0], "src"), rows_src]
+                dst = main.at[0:3, span(d[0], "dst"), rows_dst]
+                if phase == 0:
+                    copies[d + (1,)] = remote(
+                        phase,
+                        len(DIRS) + len(RELAYS) + i,
+                        main.at[3:7, span(d[0], "src", 3), span(d[1], "src", 3)],
+                        main.at[3:7, span(d[0], "dst", 3), span(d[1], "dst", 3)],
+                        d,
+                    )
             elif d[0] == 0:
                 src = sides[4].at[0 if d[2] > 0 else 1, :, :, slice(rows_src.start - H, rows_src.stop - H)]
                 dst = received.at[1 if d[2] > 0 else 0, :, :, rows_dst]
@@ -231,9 +239,9 @@
                 dst = got.at[1 if d[2] > 0 else 0, h, :, rows_dst]
             copies[d] = remote(phase, i, src, dst, d)
         turns = [(0, 1, 1), (1, 0, 1), (1, 1, 0), (0, 1, 0), (0, 0, 1), (1, 0, 0)]
-        rank = lambda d: turns.index(tuple(map(abs, d)))
-        for d in sorted(DIRS, key=rank):
-            pl.when(exists(d))(copies[d].start)
+        rank = lambda d: turns.index(tuple(map(abs, d[:3])))
+        for d in sorted(copies, key=rank):
+            pl.when(exists(d[:3]))(copies[d].start)
         return copies
 
     def relay(phase, copies, received, sides, fields):
@@ -262,7 +270,7 @@
 
     def finish(copies):
         for d, copy in copies.items():
-            way = d if len(d) == 3 else (d[0], 0, 0)
+            way = d[:3] if len(d) >= 3 else (d[0], 0, 0)
             if len(d) == 2 or d[0] or not (d[1] and d[2]):
                 pl.when(exists(opposite(way)))(copy.wait_recv)
             pl.when(exists(way))(copy.wait_send)
@@ -608,8 +616,8 @@
                 *across(2),
                 *across(1),
                 pltpu.SemaphoreType.DMA((4,)),
-                pltpu.SemaphoreType.DMA((2, len(DIRS) + len(RELAYS))),
-                pltpu.SemaphoreType.DMA((2, len(DIRS) + len(RELAYS))),
+                pltpu.SemaphoreType.DMA((2, 2 * len(DIRS) + len(RELAYS))),
+                pltpu.SemaphoreType.DMA((2, 2 * len(DIRS) + len(RELAYS))),
             ],
             compiler_params=pltpu.CompilerParams(
                 collective_id=0, has_side_effects=True, vmem_limit_bytes=63 * 1024 * 1024

time: 36.8 us -> 36.4 us (0.989)
  Pallas kernels: 34.9 us -> 34.5 us
    pallas_call x1, Pallas kernels: 34.9 us -> 34.5 us  [on_device(): pl.pallas_call(functools.partial(kernel, sizes), out_shape=jax.ShapeDtype...]
where the time goes in v4:
time: 36.4 us; the launch traced here: 36.3 us
  Pallas kernels  34.5 us (95%)
  local copies, waits for them, and re-layouts  1.77 us (5%)
    pallas_call x1, Pallas kernels, on_device(): pl.pallas_call(functools.partial(kernel, sizes), out_shape=jax.ShapeDtype...  34.5 us
    unnamed x1, local copies, waits for them, and re-layouts  1.77 us

profile of v4, /device:TPU:1, one launch (start us, length us, event | category | flops | bytes accessed | tf_op | source)
XLA Modules:
  0.0 36.3 jit_solution(570703450249666571)
XLA Ops:
  0.0 34.5 %shard_map.46 = f32[3,16,16,128]{3,2,1,0:T(8,128)} custom-call(f32[3,16,16,128]{3,2,1,0:T(8,128)} %r_hbm.1, s32[16,16,128]{2,1,0:T(8,128)} %lab_hbm.1, s32[3,16,16,128]{3,2,1,0:T(8,128)} %col_hbm.1, f32[16]{0:T(128)} %tab_hbm.1), custom_call_target="tpu_custom_call" | custom-call | flops 100000000 | bytes 2000000 | tf_op jit(solution)/shard_map/pallas_call | solution.py:584
  34.5 1.8 %copy.6 = f32[3,16,16,128]{3,2,1,0:T(8,128)} copy(f32[3,16,16,128]{3,2,1,0:T(8,128)} %shard_map.46) | data formatting | bytes 786432

commit v5 on v4

--- a/solution.py
+++ b/solution.py
@@ -492,8 +492,8 @@
 
         low, high = n + 1, B - n
 
-        @pl.loop(0, 4)
-        def _(f, keep_part=keep_part, new_part=new_part, low=low, high=high):
+        @pl.loop(0, 4, unroll=2)
+        def _(f, keep_part=keep_part, new_part=new_part, low=low, high=high, more=n + 1 < NCHEB):
             mass = jnp.where(f > 0, 1.0, 0.0)
             wxp = W[3, low - 1] * (ND[f, low] - ND[f, low - 1])
             for i in range(low, high, NBATCH):
@@ -522,8 +522,9 @@
                     res = NR[f, xp] - applied
                     inside = (row_mask * x_mask(xp)) > 0.0
                     new = jnp.where(inside, keep_part * d + new_part * res, 0.0)
-                    NR[f, xp] = res
-                    ND[f, xp] = new
+                    if more:
+                        NR[f, xp] = res
+                        ND[f, xp] = new
                     NY[f, xp] = NY[f, xp] + new
 
         if n == 1:

time: 36.4 us -> 36.4 us (level)
  no operation moved by 1% of the time
where the time goes in v5:
time: 36.4 us; the launch traced here: 36.2 us
  Pallas kernels  34.4 us (95%)
  local copies, waits for them, and re-layouts  1.77 us (5%)
    pallas_call x1, Pallas kernels, on_device(): pl.pallas_call(functools.partial(kernel, sizes), out_shape=jax.ShapeDtype...  34.4 us
    unnamed x1, local copies, waits for them, and re-layouts  1.77 us

profile of v5, /device:TPU:1, one launch (start us, length us, event | category | flops | bytes accessed | tf_op | source)
XLA Modules:
  0.0 36.2 jit_solution(12727560536597625696)
XLA Ops:
  0.0 34.4 %shard_map.46 = f32[3,16,16,128]{3,2,1,0:T(8,128)} custom-call(f32[3,16,16,128]{3,2,1,0:T(8,128)} %r_hbm.1, s32[16,16,128]{2,1,0:T(8,128)} %lab_hbm.1, s32[3,16,16,128]{3,2,1,0:T(8,128)} %col_hbm.1, f32[16]{0:T(128)} %tab_hbm.1), custom_call_target="tpu_custom_call" | custom-call | flops 100000000 | bytes 2000000 | tf_op jit(solution)/shard_map/pallas_call | solution.py:585
  34.4 1.8 %copy.6 = f32[3,16,16,128]{3,2,1,0:T(8,128)} copy(f32[3,16,16,128]{3,2,1,0:T(8,128)} %shard_map.46) | data formatting | bytes 786432
